TPU v7x, 128 devices: a whole 4x4x4 slice. The times are simulated.
128 devices in a mesh: tile: 16 (over y_lo, x, core), mp: 8 (over y_hi, z).
Axes of the slice: x: 4, y: 4 (y_hi: 2, y_lo: 2; y = y_hi * 2 + y_lo), z: 4, core: 2. Of those that a mesh axis runs over, the one named last changes fastest.
Arguments:
- tokens: bfloat16 [128, 256, 1024], P('tile', 'mp'), may hold values from -6 to 6
- ln_gain_one: float32 [1024], replicated, may hold values from 0.5 to 1.5
- ln_gain_two: float32 [1024], replicated, may hold values from 0.5 to 1.5
- qkv_weight: bfloat16 [3, 1024, 1024], P(None, None, 'mp'), may hold values from -2 to 2
- out_weight: bfloat16 [1024, 1024], P('mp'), may hold values from -0.1875 to 0.1875
- in_weight: bfloat16 [4096, 1024], P('mp'), may hold values from -0.1875 to 0.1875
- mlp_out_weight: bfloat16 [4096, 1024], P('mp'), may hold values from -0.09375 to 0.09375
- proj_weight: bfloat16 [1024, 256], replicated, may hold values from -0.1875 to 0.1875
- land_mask: int32 [128], P('tile'), may hold values 0 or 1
- placement: int32 [128], replicated, may hold values from 0 to 127, as said below
- guide: bfloat16 [512, 256, 256], P(('tile', 'mp')), may hold values from -6 to 6
- conv_weights: bfloat16 [3, 3, 3, 256, 256], replicated, may hold values from -0.125 to 0.125
- conv_bias: float32 [3, 256], replicated, may hold values from -3 to 3
Outputs:
- dense_map: bfloat16 [512, 256, 256], P(('tile', 'mp'))
Inputs may be any that keep to these rules, and one draw needn't show every extreme that they name: placement is a permutation of the scene positions; the tiles of one group land in different slabs (entry // 8), so each slab receives at most one tile of each group.
All inputs are finite; a program needn't handle non-finite values. No bound on the sum of `land_mask` on one device may be relied on, other than what follows from the above.
Results may differ from a plain program's by a relative error of at most 0.018.
The roundings to bfloat16 on the way count: a program that leaves them out, or rounds other values in their place, can miss the bound.
Values may be sent and summed in bfloat16 or wider, within the bound.
No kernel may reach another device: no remote copies, remote signals or barrier semaphores. Data moves between devices by JAX's collectives and lax.ppermute only.
A program may use at most 128 MiB of HBM per device.

v0:
```python
import jax
import jax.numpy as jnp
from jax import lax
from jax.sharding import PartitionSpec as P

HEAD = 64
SIDE = 16
UP = 2
PATCHES = 256


def extended_2(block, sides, width):
    for axis, dim in sides:
        count = lax.axis_size(axis)
        forward = [(i, i + 1) for i in range(count - 1)]
        backward = [(target, source) for source, target in forward]
        low = lax.ppermute(
            lax.slice_in_dim(block, block.shape[dim] - width, None, axis=dim), axis, forward
        )
        high = lax.ppermute(lax.slice_in_dim(block, 0, width, axis=dim), axis, backward)
        block = jnp.concatenate([low, block, high], axis=dim)
    return block


def layer_norm(values, gain):
    widened = values.astype(jnp.float32)
    centre = jnp.mean(widened, axis=-1, keepdims=True)
    spread = jnp.mean((widened - centre) ** 2, axis=-1, keepdims=True)
    return ((widened - centre) * lax.rsqrt(spread + 1e-06) * gain).astype(jnp.bfloat16)


def conv_layer(extended, kernel, shift, out_count):
    width_px = extended.shape[1]
    padded = jnp.pad(extended, ((0, 0), (1, 1), (0, 0)))
    running = jnp.zeros((out_count, width_px, kernel.shape[-1]), jnp.float32) + shift
    for row_shift in range(3):
        for col_shift in range(3):
            window = padded[row_shift : row_shift + out_count, col_shift : col_shift + width_px]
            running = running + jnp.einsum(
                "rwc,cd->rwd",
                window,
                kernel[row_shift, col_shift],
                preferred_element_type=jnp.float32,
            )
    return running


def per_device(
    tokens,
    ln_gain_one,
    ln_gain_two,
    qkv_weight,
    out_weight,
    in_weight,
    mlp_out_weight,
    proj_weight,
    land_mask,
    placement,
    guide,
    conv_weights,
    conv_bias,
):
    tiles_here = tokens.shape[0]
    seg_rows = tokens.shape[1]
    groups = lax.axis_size("tile")
    normed = layer_norm(tokens, ln_gain_one)
    gathered = lax.all_gather(normed, "mp", axis=1, tiled=True)
    projected = jnp.einsum(
        "tpd,kde->ktpe", gathered, qkv_weight, preferred_element_type=jnp.float32
    ).astype(jnp.bfloat16)
    heads_local = projected.shape[-1] // HEAD
    shaped = projected.reshape(3, tiles_here, PATCHES, heads_local, HEAD)
    scores = jnp.einsum(
        "tphe,tqhe->thpq", shaped[0], shaped[1], preferred_element_type=jnp.float32
    ) * HEAD ** (-0.5)
    soft_weights = jax.nn.softmax(scores, axis=-1).astype(jnp.bfloat16)
    context = jnp.einsum(
        "thpq,tqhe->tphe", soft_weights, shaped[2], preferred_element_type=jnp.float32
    )
    context = context.astype(jnp.bfloat16).reshape(tiles_here, PATCHES, heads_local * HEAD)
    partial_value = jnp.einsum(
        "tpe,ed->tpd", context, out_weight, preferred_element_type=jnp.float32
    )
    attention = lax.psum_scatter(
        partial_value.astype(jnp.bfloat16), "mp", scatter_dimension=1, tiled=True
    ).astype(jnp.float32)
    middle = (tokens.astype(jnp.float32) + attention).astype(jnp.bfloat16)
    normed_mid = layer_norm(middle, ln_gain_two)
    gathered_mid = lax.all_gather(normed_mid, "mp", axis=1, tiled=True)
    hidden = jnp.einsum("tpd,fd->tpf", gathered_mid, in_weight, preferred_element_type=jnp.float32)
    hidden = jax.nn.gelu(hidden).astype(jnp.bfloat16)
    mlp_terms = jnp.einsum(
        "tpf,fd->tpd", hidden, mlp_out_weight, preferred_element_type=jnp.float32
    )
    mlp_part = lax.psum_scatter(
        mlp_terms.astype(jnp.bfloat16), "mp", scatter_dimension=1, tiled=True
    ).astype(jnp.float32)
    features = (middle.astype(jnp.float32) + mlp_part).astype(jnp.bfloat16)
    mask_here = land_mask.astype(jnp.bfloat16)[:, None, None]
    group_here = lax.axis_index("tile")
    slab_all = placement // tiles_here
    column_all = placement % tiles_here
    group_all = jnp.arange(placement.shape[0], dtype=jnp.int32) // tiles_here
    slab_local = lax.dynamic_slice_in_dim(slab_all, group_here * tiles_here, tiles_here, 0)
    selector = (slab_local[None, :] == jnp.arange(groups, dtype=jnp.int32)[:, None]).astype(
        jnp.bfloat16
    )
    in_slab = slab_all == group_here
    column_hot = (
        column_all[:, None] == jnp.arange(tiles_here, dtype=jnp.int32)[None, :]
    ) & in_slab[:, None]
    group_hot = group_all[:, None] == jnp.arange(groups, dtype=jnp.int32)[None, :]
    arrange = jnp.einsum(
        "tk,tg->kg", column_hot.astype(jnp.float32), group_hot.astype(jnp.float32)
    ).astype(jnp.bfloat16)
    masked = features * mask_here
    outgoing = jnp.einsum(
        "sj,jpd->spd", selector, masked, preferred_element_type=jnp.float32
    ).astype(jnp.bfloat16)
    incoming = lax.all_to_all(outgoing, "tile", split_axis=0, concat_axis=0, tiled=True)
    slab_feats = jnp.einsum(
        "kg,gpd->kpd", arrange, incoming, preferred_element_type=jnp.float32
    ).astype(jnp.bfloat16)
    slab_embed = jnp.einsum(
        "kpd,dc->kpc", slab_feats, proj_weight, preferred_element_type=jnp.float32
    )
    slab_embed = slab_embed.astype(jnp.bfloat16)
    token_rows = seg_rows // SIDE
    channels = proj_weight.shape[1]
    image = slab_embed.reshape(tiles_here, token_rows, SIDE, channels)
    image = jnp.transpose(image, (1, 0, 2, 3)).reshape(token_rows, tiles_here * SIDE, channels)
    upsampled = jnp.repeat(jnp.repeat(image, UP, axis=0), UP, axis=1)
    guided = (upsampled.astype(jnp.float32) + guide.astype(jnp.float32)).astype(jnp.bfloat16)
    row_count = guided.shape[0]

    def section(values, layer):
        widened = extended_2(values, ((("tile", "mp"), 0),), 1)
        return conv_layer(widened, conv_weights[layer], conv_bias[layer], row_count)

    first = jax.nn.gelu(section(guided, 0)).astype(jnp.bfloat16)
    second = jax.nn.gelu(section(first, 1)).astype(jnp.bfloat16)
    last_term = section(second, 2)
    return (guided.astype(jnp.float32) + last_term).astype(jnp.bfloat16)


def solution(mesh):
    in_specs = (
        P("tile", "mp", None),
        P(),
        P(),
        P(None, None, "mp"),
        P("mp", None),
        P("mp", None),
        P("mp", None),
        P(),
        P("tile"),
        P(),
        P(("tile", "mp"), None, None),
        P(),
        P(),
    )
    out_specs = P(("tile", "mp"), None, None)
    return jax.shard_map(
        per_device, mesh=mesh, in_specs=in_specs, out_specs=out_specs, check_vma=False
    )
```

profile of v0, /device:TPU:1, one launch (start us, length us, event | category | flops | bytes accessed | tf_op | source)
XLA Modules:
  0.0 432.7 jit_solution(2327485380840038039)
XLA Ops:
  6.5 1.3 convert_reduce_fusion.1
  7.9 1.3 fusion.59
  9.2 2.1 fusion.61
  11.4 74.5 %all-gather.3.cloned.1.call-done = bf16[8,256,1024]{2,1,0:T(8,128)(2,1)} async-done(((bf16[8,32,1024]{2,1,0:T(8,128)(2,1)}), bf16[8,256,1024]{2,1,0:T(8,128)(2,1)}) %all-gather.3.cloned.1.call-update) | async-done | bytes 4194320 | tf_op jit(solution)/shard_map/all_gather | solution.py:67
  85.9 4.0 fusion.25
  90.1 3.5 fusion.186
  93.6 2.7 fusion.48
  96.3 3.2 convolution_convert_fusion.1
  99.7 81.9 %reduce-scatter.3.cloned.1.call-done = bf16[8,32,1024]{2,1,0:T(8,128)(2,1)} async-done(((bf16[8,256,1024]{2,1,0:T(8,128)(2,1)}), bf16[8,32,1024]{2,1,0:T(8,128)(2,1)}) %reduce-scatter.3.cloned.1.call-update) | async-done | bytes 524304 | tf_op jit(solution)/shard_map/reduce_scatter | solution.py:84
  181.6 1.3 convert_reduce_fusion
  183.1 1.1 fusion.58
  184.3 71.1 %all-gather.5.cloned.1.call-done = bf16[8,256,1024]{2,1,0:T(8,128)(2,1)} async-done(((bf16[8,32,1024]{2,1,0:T(8,128)(2,1)}), bf16[8,256,1024]{2,1,0:T(8,128)(2,1)}) %all-gather.5.cloned.1.call-update) | async-done | bytes 4194320 | tf_op jit(solution)/shard_map/all_gather | solution.py:89
  255.4 8.2 %convolution_convert_fusion = bf16[8,256,1024]{2,1,0:T(8,128)(2,1)} fusion(bf16[8,256,1024]{2,1,0:T(8,128)(2,1)} %all-gather.5.cloned.1.call-done, bf16[512,1024]{1,0:T(8,128)(2,1)S(1)} %copy-done, bf16[512,1024]{1,0:T(8,128)(2,1)S(1)} %copy-done.8), kind=kOutput, calls=%fused_computation.16 | convolution fusion | flops 4306501632 | bytes 10485760 | tf_op jit(solution)/shard_map/tpf,fd->tpd/dot_general | solution.py:92
  263.6 0.6 copy-done.10
  264.4 81.3 %reduce-scatter.5.cloned.1.call-done = bf16[8,32,1024]{2,1,0:T(8,128)(2,1)} async-done(((bf16[8,256,1024]{2,1,0:T(8,128)(2,1)}), bf16[8,32,1024]{2,1,0:T(8,128)(2,1)}) %reduce-scatter.5.cloned.1.call-update) | async-done | bytes 524304 | tf_op jit(solution)/shard_map/reduce_scatter | solution.py:95
  345.7 1.3 fusion.114
  346.9 0.5 fusion.149
  347.4 1.5 copy.37
  349.0 6.1 %all-to-all-start = ((bf16[16,32,1024]{2,1,0:T(8,128)(2,1)}), bf16[16,32,1024]{2,1,0:T(8,128)(2,1)S(1)}, u32[]{:S(2)}, u32[]{:S(2)}) async-start(bf16[16,32,1024]{2,1,0:T(8,128)(2,1)} %copy.37), calls=%async_computation.2 | async-start | bytes 2097152 | tf_op jit(solution)/shard_map/all_to_all | solution.py:120
  355.1 3.3 slice_bitcast_fusion
  358.4 12.5 %all-to-all-done = bf16[16,32,1024]{2,1,0:T(8,128)(2,1)S(1)} async-done(((bf16[16,32,1024]{2,1,0:T(8,128)(2,1)}), bf16[16,32,1024]{2,1,0:T(8,128)(2,1)S(1)}, u32[]{:S(2)}, u32[]{:S(2)}) %all-to-all-start) | async-done | bytes 1048608 | tf_op jit(solution)/shard_map/all_to_all | solution.py:120
  370.9 1.7 fusion.83
  372.6 1.7 convolution_convert_fusion.2
  374.3 0.4 broadcast_in_dim.5
  374.7 1.7 convert_element_type.132
  376.4 1.6 add_convert_fusion
  378.0 2.9 collective-permute-start
  380.8 6.3 %collective-permute-start.1 = (bf16[1,256,256]{2,1,0:T(8,128)(2,1)S(1)}, bf16[1,256,256]{2,1,0:T(8,128)(2,1)S(1)}, u32[]{:S(2)}, u32[]{:S(2)}) collective-permute-start(bf16[1,256,256]{2,1,0:T(8,128)(2,1)S(1)} %get-tuple-element.20), channel_id=1, source_target_pairs={{1,0},{2,1},{3,2},{4,3},{5,4},{6,5},{7,6},{8,7},{9,8},{10,9},{11,1... | collective-permute-start | bytes 393224 | tf_op jit(solution)/shard_map/ppermute | solution.py:20
  387.5 0.4 collective-permute-done
  387.9 2.6 collective-permute-done.1
  391.0 0.3 fusion.141
  391.6 0.3 fusion.145
  391.9 0.3 fusion.137
  392.5 0.5 fusion.46
  393.0 0.6 fusion.71
  393.6 1.9 collective-permute-start.2
  395.6 8.0 %collective-permute-start.3 = (bf16[1,256,256]{2,1,0:T(8,128)(2,1)S(1)}, bf16[1,256,256]{2,1,0:T(8,128)(2,1)S(1)}, u32[]{:S(2)}, u32[]{:S(2)}) collective-permute-start(bf16[1,256,256]{2,1,0:T(8,128)(2,1)S(1)} %get-tuple-element.18), channel_id=1, source_target_pairs={{1,0},{2,1},{3,2},{4,3},{5,4},{6,5},{7,6},{8,7},{9,8},{10,9},{11,1... | collective-permute-start | bytes 393224 | tf_op jit(solution)/shard_map/ppermute | solution.py:20
  403.9 0.4 collective-permute-done.2
  404.3 2.3 collective-permute-done.3
  408.6 0.5 fusion.40
  409.1 0.6 fusion.79
  409.7 1.9 collective-permute-start.4
  411.6 8.0 %collective-permute-start.5 = (bf16[1,256,256]{2,1,0:T(8,128)(2,1)S(1)}, bf16[1,256,256]{2,1,0:T(8,128)(2,1)S(1)}, u32[]{:S(2)}, u32[]{:S(2)}) collective-permute-start(bf16[1,256,256]{2,1,0:T(8,128)(2,1)S(1)} %get-tuple-element.16), channel_id=1, source_target_pairs={{1,0},{2,1},{3,2},{4,3},{5,4},{6,5},{7,6},{8,7},{9,8},{10,9},{11,1... | collective-permute-start | bytes 393224 | tf_op jit(solution)/shard_map/ppermute | solution.py:20
  419.9 0.4 collective-permute-done.4
  420.3 2.2 collective-permute-done.5
  423.0 0.3 fusion.123
  424.6 0.5 fusion.34
  425.1 1.1 fusion.47
  (65 shorter events, 6.6 us)
Async XLA Ops:
  6.5 248.8 %copy-start = (bf16[512,1024]{1,0:T(8,128)(2,1)S(1)}, bf16[512,1024]{1,0:T(8,128)(2,1)}, u32[]{:S(2)}) copy-start(bf16[512,1024]{1,0:T(8,128)(2,1)} %param.19) | copy-start | bytes 3145732
  6.5 79.4 %copy-start.9 = (bf16[3,1024,128]{2,1,0:T(8,128)(2,1)S(1)}, bf16[3,1024,128]{2,1,0:T(8,128)(2,1)}, u32[]{:S(2)}) copy-start(bf16[3,1024,128]{2,1,0:T(8,128)(2,1)} %param.16) | copy-start | bytes 2359300
  6.5 79.4 %all-gather.3.cloned.1.call-start = ((), (), s32[]{:S(2)}) async-start(), calls=%async_computation.3 | async-start | bytes 4718592 | tf_op jit(solution)/shard_map/all_gather | solution.py:67
  11.4 170.2 %reduce-scatter.3.cloned.1.call-start = ((), (), s32[]{:S(2)}) async-start(), calls=%async_computation.4 | async-start | bytes 4718592 | tf_op jit(solution)/shard_map/reduce_scatter | solution.py:84
  93.6 2.7 copy-start.4
  99.6 82.0 %copy-start.2 = (bf16[8,32,1024]{2,1,0:T(8,128)(2,1)S(1)}, bf16[8,32,1024]{2,1,0:T(8,128)(2,1)}, u32[]{:S(2)}) copy-start(bf16[8,32,1024]{2,1,0:T(8,128)(2,1)} %param.13) | copy-start | bytes 1572868
  99.6 83.5 %copy-start.5 = (f32[1024]{0:T(1024)S(1)}, f32[1024]{0:T(1024)}, u32[]{:S(2)}) copy-start(f32[1024]{0:T(1024)} %param.15) | copy-start | bytes 12292
  99.6 155.8 %copy-start.8 = (bf16[512,1024]{1,0:T(8,128)(2,1)S(1)}, bf16[512,1024]{1,0:T(8,128)(2,1)}, u32[]{:S(2)}) copy-start(bf16[512,1024]{1,0:T(8,128)(2,1)} %param.18) | copy-start | bytes 3145732
  99.6 155.8 %all-gather.5.cloned.1.call-start = ((), (), s32[]{:S(2)}) async-start(), calls=%async_computation.5 | async-start | bytes 4718592 | tf_op jit(solution)/shard_map/all_gather | solution.py:89
  184.3 161.4 %reduce-scatter.5.cloned.1.call-start = ((), (), s32[]{:S(2)}) async-start(), calls=%async_computation.6 | async-start | bytes 4718592 | tf_op jit(solution)/shard_map/reduce_scatter | solution.py:95
  263.6 0.7 copy-start.10
  263.6 0.7 copy-start.7
  349.0 6.1 %copy-start.6 = (f32[3,256]{1,0:T(4,128)S(1)}, f32[3,256]{1,0:T(4,128)}, u32[]{:S(2)}) copy-start(f32[3,256]{1,0:T(4,128)} %param.25) | copy-start | bytes 9220
  349.0 21.9 %all-to-all-start = ((bf16[16,32,1024]{2,1,0:T(8,128)(2,1)}), bf16[16,32,1024]{2,1,0:T(8,128)(2,1)S(1)}, u32[]{:S(2)}, u32[]{:S(2)}) async-start(bf16[16,32,1024]{2,1,0:T(8,128)(2,1)} %copy.37), calls=%async_computation.2 | async-start | bytes 2097152 | tf_op jit(solution)/shard_map/all_to_all | solution.py:120
  376.4 10.8 %copy-start.3 = (bf16[3,3,256,256]{3,2,1,0:T(8,128)(2,1)S(1)}, bf16[3,3,256,256]{3,2,1,0:T(8,128)(2,1)}, u32[]{:S(2)}) copy-start(bf16[3,3,256,256]{3,2,1,0:T(8,128)(2,1)} %get-tuple-element.10) | copy-start | bytes 3538948
  378.0 9.9 %collective-permute-start = (bf16[1,256,256]{2,1,0:T(8,128)(2,1)S(1)}, bf16[1,256,256]{2,1,0:T(8,128)(2,1)S(1)}, u32[]{:S(2)}, u32[]{:S(2)}) collective-permute-start(bf16[1,256,256]{2,1,0:T(8,128)(2,1)S(1)} %get-tuple-element.19), channel_id=1, source_target_pairs={{0,1},{1,2},{2,3},{3,4},{4,5},{5,6},{6,7},{7,8},{8,9},{9,10},{10,1... | collective-permute-start | bytes 393224 | tf_op jit(solution)/shard_map/ppermute | solution.py:17
  380.8 9.6 %collective-permute-start.1 = (bf16[1,256,256]{2,1,0:T(8,128)(2,1)S(1)}, bf16[1,256,256]{2,1,0:T(8,128)(2,1)S(1)}, u32[]{:S(2)}, u32[]{:S(2)}) collective-permute-start(bf16[1,256,256]{2,1,0:T(8,128)(2,1)S(1)} %get-tuple-element.20), channel_id=1, source_target_pairs={{1,0},{2,1},{3,2},{4,3},{5,4},{6,5},{7,6},{8,7},{9,8},{10,9},{11,1... | collective-permute-start | bytes 393224 | tf_op jit(solution)/shard_map/ppermute | solution.py:20
  393.6 10.6 %collective-permute-start.2 = (bf16[1,256,256]{2,1,0:T(8,128)(2,1)S(1)}, bf16[1,256,256]{2,1,0:T(8,128)(2,1)S(1)}, u32[]{:S(2)}, u32[]{:S(2)}) collective-permute-start(bf16[1,256,256]{2,1,0:T(8,128)(2,1)S(1)} %get-tuple-element.17), channel_id=1, source_target_pairs={{0,1},{1,2},{2,3},{3,4},{4,5},{5,6},{6,7},{7,8},{8,9},{9,10},{10,1... | collective-permute-start | bytes 393224 | tf_op jit(solution)/shard_map/ppermute | solution.py:17
  395.6 11.0 %collective-permute-start.3 = (bf16[1,256,256]{2,1,0:T(8,128)(2,1)S(1)}, bf16[1,256,256]{2,1,0:T(8,128)(2,1)S(1)}, u32[]{:S(2)}, u32[]{:S(2)}) collective-permute-start(bf16[1,256,256]{2,1,0:T(8,128)(2,1)S(1)} %get-tuple-element.18), channel_id=1, source_target_pairs={{1,0},{2,1},{3,2},{4,3},{5,4},{6,5},{7,6},{8,7},{9,8},{10,9},{11,1... | collective-permute-start | bytes 393224 | tf_op jit(solution)/shard_map/ppermute | solution.py:20
  409.7 10.6 %collective-permute-start.4 = (bf16[1,256,256]{2,1,0:T(8,128)(2,1)S(1)}, bf16[1,256,256]{2,1,0:T(8,128)(2,1)S(1)}, u32[]{:S(2)}, u32[]{:S(2)}) collective-permute-start(bf16[1,256,256]{2,1,0:T(8,128)(2,1)S(1)} %get-tuple-element.15), channel_id=1, source_target_pairs={{0,1},{1,2},{2,3},{3,4},{4,5},{5,6},{6,7},{7,8},{8,9},{9,10},{10,1... | collective-permute-start | bytes 393224 | tf_op jit(solution)/shard_map/ppermute | solution.py:17
  411.6 10.9 %collective-permute-start.5 = (bf16[1,256,256]{2,1,0:T(8,128)(2,1)S(1)}, bf16[1,256,256]{2,1,0:T(8,128)(2,1)S(1)}, u32[]{:S(2)}, u32[]{:S(2)}) collective-permute-start(bf16[1,256,256]{2,1,0:T(8,128)(2,1)S(1)} %get-tuple-element.16), channel_id=1, source_target_pairs={{1,0},{2,1},{3,2},{4,3},{5,4},{6,5},{7,6},{8,7},{9,8},{10,9},{11,1... | collective-permute-start | bytes 393224 | tf_op jit(solution)/shard_map/ppermute | solution.py:20
  424.6 1.6 copy-start.1
Sparse Core Ops, SparseCore 0:
  11.5 74.3 all-gather.2
  99.7 81.7 reduce-scatter.2
  184.4 70.9 all-gather.4
  263.7 81.8 reduce-scatter.4
where the time goes:
time: 433 us
  waiting for transfers between devices  330 us (76%)
  matrix products  35.6 us (8%)
  starting transfers between devices  35.2 us (8%)
  between operations  13.5 us (3%)
  other arithmetic  10.9 us (3%)
  local copies, waits for them, and re-layouts  7.92 us (2%)
    reduce_scatter x1, waiting for transfers between devices, per_device(): lax.psum_scatter(partial_value.astype(jnp.bfloat16), 'mp', scatter_dimens...  81.9 us
    reduce_scatter x1, waiting for transfers between devices, per_device(): lax.psum_scatter(mlp_terms.astype(jnp.bfloat16), 'mp', scatter_dimension=...  81.3 us
    all_gather x1, waiting for transfers between devices, per_device(): gathered = lax.all_gather(normed, 'mp', axis=1, tiled=True)  74.5 us
    all_gather x1, waiting for transfers between devices, per_device(): gathered_mid = lax.all_gather(normed_mid, 'mp', axis=1, tiled=True)  71.1 us
    ppermute x3, starting transfers between devices, extended_2(): lax.ppermute(lax.slice_in_dim(block, 0, width, axis=dim), axis, backward)  22.3 us
    all_to_all x1, waiting for transfers between devices, per_device(): lax.all_to_all(outgoing, 'tile', split_axis=0, concat_axis=0, tiled=True)  12.5 us
    dot_general x27, matrix products, conv_layer(): jnp.einsum('rwc,cd->rwd', window, kernel[row_shift, col_shift], preferred...  10.1 us
  transfers between devices with their start and end apart: 11, of which 11 were waited for; matrix products, arithmetic and copies ran while one was open for 1% of the time, Pallas kernels for 0%

commit v1 on v0

--- a/solution.py
+++ b/solution.py
@@ -86,7 +86,9 @@
     ).astype(jnp.float32)
     middle = (tokens.astype(jnp.float32) + attention).astype(jnp.bfloat16)
     normed_mid = layer_norm(middle, ln_gain_two)
-    gathered_mid = lax.all_gather(normed_mid, "mp", axis=1, tiled=True)
+    gathered_mid = jnp.concatenate(
+        lax.all_to_all(jnp.stack([normed_mid] * lax.axis_size("mp")), "mp", 0, 0), axis=1
+    )
     hidden = jnp.einsum("tpd,fd->tpf", gathered_mid, in_weight, preferred_element_type=jnp.float32)
     hidden = jax.nn.gelu(hidden).astype(jnp.bfloat16)
     mlp_terms = jnp.einsum(

time: 433 us -> 417 us (0.963)
  waiting for transfers between devices: 330 us -> 262 us
  blocking collectives: 0 us -> 49.9 us
    all_gather x1 -> x0, waiting for transfers between devices: 71.1 us -> none  [per_device(): gathered_mid = lax.all_gather(normed_mid, 'mp', axis=1, tiled=True)]
    all_to_all x0 -> x1, blocking collectives: none -> 49.9 us  [per_device(): lax.all_to_all(jnp.stack([normed_mid] * lax.axis_size('mp')), 'mp', 0, 0)]
  transfers between devices with their start and end apart: 11 -> 10, of which waited for: 11 -> 10; matrix products, arithmetic and copies ran while one was open for 1% -> 1% of each run, Pallas kernels for 0% -> 0%
where the time goes in v1:
time: 417 us
  waiting for transfers between devices  262 us (63%)
  blocking collectives  49.9 us (12%)
  matrix products  35.7 us (9%)
  starting transfers between devices  35.1 us (8%)
  between operations  13.5 us (3%)
  local copies, waits for them, and re-layouts  10.9 us (3%)
  other arithmetic  10.1 us (2%)
    reduce_scatter x1, waiting for transfers between devices, per_device(): lax.psum_scatter(mlp_terms.astype(jnp.bfloat16), 'mp', scatter_dimension=...  84.5 us
    reduce_scatter x1, waiting for transfers between devices, per_device(): lax.psum_scatter(partial_value.astype(jnp.bfloat16), 'mp', scatter_dimens...  81.9 us
    all_gather x1, waiting for transfers between devices, per_device(): gathered = lax.all_gather(normed, 'mp', axis=1, tiled=True)  74.5 us
    all_to_all x1, blocking collectives, per_device(): lax.all_to_all(jnp.stack([normed_mid] * lax.axis_size('mp')), 'mp', 0, 0)  49.9 us
    ppermute x3, starting transfers between devices, extended_2(): lax.ppermute(lax.slice_in_dim(block, 0, width, axis=dim), axis, backward)  22.3 us
    all_to_all x1, waiting for transfers between devices, per_device(): lax.all_to_all(outgoing, 'tile', split_axis=0, concat_axis=0, tiled=True)  12.5 us
    dot_general x27, matrix products, conv_layer(): jnp.einsum('rwc,cd->rwd', window, kernel[row_shift, col_shift], preferred...  10 us
  transfers between devices with their start and end apart: 10, of which 10 were waited for; matrix products, arithmetic and copies ran while one was open for 1% of the time, Pallas kernels for 0%

profile of v1, /device:TPU:1, one launch (start us, length us, event | category | flops | bytes accessed | tf_op | source)
XLA Modules:
  0.0 416.8 jit_solution(528101683971343547)
XLA Ops:
  6.5 1.3 convert_reduce_fusion.1
  7.9 1.3 fusion.59
  9.2 2.1 fusion.61
  11.4 74.5 %all-gather.2.cloned.1.call-done = bf16[8,256,1024]{2,1,0:T(8,128)(2,1)} async-done(((bf16[8,32,1024]{2,1,0:T(8,128)(2,1)}), bf16[8,256,1024]{2,1,0:T(8,128)(2,1)}) %all-gather.2.cloned.1.call-update) | async-done | bytes 4194320 | tf_op jit(solution)/shard_map/all_gather | solution.py:67
  85.9 4.0 fusion.25
  90.1 3.5 fusion.185
  93.6 2.7 fusion.48
  96.3 3.2 convolution_convert_fusion.1
  99.6 81.9 %reduce-scatter.3.cloned.1.call-done = bf16[8,32,1024]{2,1,0:T(8,128)(2,1)} async-done(((bf16[8,256,1024]{2,1,0:T(8,128)(2,1)}), bf16[8,32,1024]{2,1,0:T(8,128)(2,1)}) %reduce-scatter.3.cloned.1.call-update) | async-done | bytes 524304 | tf_op jit(solution)/shard_map/reduce_scatter | solution.py:84
  181.5 1.3 convert_reduce_fusion
  183.4 0.5 stack.2
  183.9 49.9 %all_to_all.10 = bf16[8,8,32,1024]{3,2,1,0:T(8,128)(2,1)S(1)} all-to-all(bf16[8,8,32,1024]{3,2,1,0:T(8,128)(2,1)S(1)} %stack.2), channel_id=1, replica_groups=mesh['tile'=16,'mp'=8] {'mp'}, dimensions={0} | all-to-all | bytes 8388608 | tf_op jit(solution)/shard_map/all_to_all | solution.py:90
  233.9 2.4 copy.31
  236.3 8.3 %convolution_convert_fusion = bf16[8,256,1024]{2,1,0:T(8,128)(2,1)} fusion(bf16[8,256,1024]{2,1,0:T(8,128)(2,1)} %bitcast.203, bf16[512,1024]{1,0:T(8,128)(2,1)S(1)} %copy-done, bf16[512,1024]{1,0:T(8,128)(2,1)S(1)} %copy-done.8), kind=kOutput, calls=%fused_computation.16 | convolution fusion | flops 4306501632 | bytes 10485760 | tf_op jit(solution)/shard_map/tpf,fd->tpd/dot_general | solution.py:94
  244.6 0.6 copy-done.10
  245.3 84.5 %reduce-scatter.5.cloned.1.call-done = bf16[8,32,1024]{2,1,0:T(8,128)(2,1)} async-done(((bf16[8,256,1024]{2,1,0:T(8,128)(2,1)}), bf16[8,32,1024]{2,1,0:T(8,128)(2,1)}) %reduce-scatter.5.cloned.1.call-update) | async-done | bytes 524304 | tf_op jit(solution)/shard_map/reduce_scatter | solution.py:97
  329.8 1.3 fusion.113
  331.0 0.6 convolution_convert_fusion.2
  331.6 1.5 copy.33
  333.2 6.0 %all-to-all-start.1 = ((bf16[16,32,1024]{2,1,0:T(8,128)(2,1)}), bf16[16,32,1024]{2,1,0:T(8,128)(2,1)S(1)}, u32[]{:S(2)}, u32[]{:S(2)}) async-start(bf16[16,32,1024]{2,1,0:T(8,128)(2,1)} %copy.33), calls=%async_computation.3 | async-start | bytes 2097152 | tf_op jit(solution)/shard_map/all_to_all | solution.py:122
  339.2 3.3 slice_bitcast_fusion
  342.5 12.5 %all-to-all-done.1 = bf16[16,32,1024]{2,1,0:T(8,128)(2,1)S(1)} async-done(((bf16[16,32,1024]{2,1,0:T(8,128)(2,1)}), bf16[16,32,1024]{2,1,0:T(8,128)(2,1)S(1)}, u32[]{:S(2)}, u32[]{:S(2)}) %all-to-all-start.1) | async-done | bytes 1048608 | tf_op jit(solution)/shard_map/all_to_all | solution.py:122
  355.0 1.7 convolution_convert_fusion.3
  356.7 1.7 convolution_convert_fusion.4
  358.4 0.4 broadcast_in_dim.5
  358.8 1.7 convert_element_type.132
  360.5 1.6 add_convert_fusion
  362.1 2.9 collective-permute-start
  365.0 6.2 %collective-permute-start.1 = (bf16[1,256,256]{2,1,0:T(8,128)(2,1)S(1)}, bf16[1,256,256]{2,1,0:T(8,128)(2,1)S(1)}, u32[]{:S(2)}, u32[]{:S(2)}) collective-permute-start(bf16[1,256,256]{2,1,0:T(8,128)(2,1)S(1)} %get-tuple-element.20), channel_id=1, source_target_pairs={{1,0},{2,1},{3,2},{4,3},{5,4},{6,5},{7,6},{8,7},{9,8},{10,9},{11,1... | collective-permute-start | bytes 393224 | tf_op jit(solution)/shard_map/ppermute | solution.py:20
  371.6 0.4 collective-permute-done
  372.0 2.6 collective-permute-done.1
  375.7 0.3 fusion.144
  376.0 0.3 fusion.136
  376.6 0.5 fusion.46
  377.1 0.6 fusion.71
  377.7 1.9 collective-permute-start.2
  379.7 8.0 %collective-permute-start.3 = (bf16[1,256,256]{2,1,0:T(8,128)(2,1)S(1)}, bf16[1,256,256]{2,1,0:T(8,128)(2,1)S(1)}, u32[]{:S(2)}, u32[]{:S(2)}) collective-permute-start(bf16[1,256,256]{2,1,0:T(8,128)(2,1)S(1)} %get-tuple-element.18), channel_id=1, source_target_pairs={{1,0},{2,1},{3,2},{4,3},{5,4},{6,5},{7,6},{8,7},{9,8},{10,9},{11,1... | collective-permute-start | bytes 393224 | tf_op jit(solution)/shard_map/ppermute | solution.py:20
  388.0 0.4 collective-permute-done.2
  388.4 2.3 collective-permute-done.3
  391.5 0.3 fusion.129
  392.7 0.5 fusion.40
  393.2 0.6 fusion.79
  393.8 1.9 collective-permute-start.4
  395.7 8.0 %collective-permute-start.5 = (bf16[1,256,256]{2,1,0:T(8,128)(2,1)S(1)}, bf16[1,256,256]{2,1,0:T(8,128)(2,1)S(1)}, u32[]{:S(2)}, u32[]{:S(2)}) collective-permute-start(bf16[1,256,256]{2,1,0:T(8,128)(2,1)S(1)} %get-tuple-element.16), channel_id=1, source_target_pairs={{1,0},{2,1},{3,2},{4,3},{5,4},{6,5},{7,6},{8,7},{9,8},{10,9},{11,1... | collective-permute-start | bytes 393224 | tf_op jit(solution)/shard_map/ppermute | solution.py:20
  404.0 0.4 collective-permute-done.4
  404.4 2.2 collective-permute-done.5
  408.7 0.5 fusion.34
  409.1 1.1 fusion.47
  (65 shorter events, 7.1 us)
Async XLA Ops:
  6.5 229.7 %copy-start = (bf16[512,1024]{1,0:T(8,128)(2,1)S(1)}, bf16[512,1024]{1,0:T(8,128)(2,1)}, u32[]{:S(2)}) copy-start(bf16[512,1024]{1,0:T(8,128)(2,1)} %param.19) | copy-start | bytes 3145732
  6.5 79.4 %copy-start.9 = (bf16[3,1024,128]{2,1,0:T(8,128)(2,1)S(1)}, bf16[3,1024,128]{2,1,0:T(8,128)(2,1)}, u32[]{:S(2)}) copy-start(bf16[3,1024,128]{2,1,0:T(8,128)(2,1)} %param.16) | copy-start | bytes 2359300
  6.5 79.4 %all-gather.2.cloned.1.call-start = ((), (), s32[]{:S(2)}) async-start(), calls=%async_computation.4 | async-start | bytes 4718592 | tf_op jit(solution)/shard_map/all_gather | solution.py:67
  11.4 170.2 %reduce-scatter.3.cloned.1.call-start = ((), (), s32[]{:S(2)}) async-start(), calls=%async_computation.5 | async-start | bytes 4718592 | tf_op jit(solution)/shard_map/reduce_scatter | solution.py:84
  93.6 2.7 copy-start.4
  99.5 82.0 %copy-start.2 = (bf16[8,32,1024]{2,1,0:T(8,128)(2,1)S(1)}, bf16[8,32,1024]{2,1,0:T(8,128)(2,1)}, u32[]{:S(2)}) copy-start(bf16[8,32,1024]{2,1,0:T(8,128)(2,1)} %param.13) | copy-start | bytes 1572868
  99.6 83.5 %copy-start.5 = (f32[1024]{0:T(1024)S(1)}, f32[1024]{0:T(1024)}, u32[]{:S(2)}) copy-start(f32[1024]{0:T(1024)} %param.15) | copy-start | bytes 12292
  99.6 230.2 %reduce-scatter.5.cloned.1.call-start = ((), (), s32[]{:S(2)}) async-start(), calls=%async_computation.6 | async-start | bytes 4718592 | tf_op jit(solution)/shard_map/reduce_scatter | solution.py:97
  233.9 2.4 copy-start.8
  244.5 0.7 copy-start.10
  244.5 0.7 copy-start.7
  333.1 6.0 %copy-start.6 = (f32[3,256]{1,0:T(4,128)S(1)}, f32[3,256]{1,0:T(4,128)}, u32[]{:S(2)}) copy-start(f32[3,256]{1,0:T(4,128)} %param.25) | copy-start | bytes 9220
  333.2 21.9 %all-to-all-start.1 = ((bf16[16,32,1024]{2,1,0:T(8,128)(2,1)}), bf16[16,32,1024]{2,1,0:T(8,128)(2,1)S(1)}, u32[]{:S(2)}, u32[]{:S(2)}) async-start(bf16[16,32,1024]{2,1,0:T(8,128)(2,1)} %copy.33), calls=%async_computation.3 | async-start | bytes 2097152 | tf_op jit(solution)/shard_map/all_to_all | solution.py:122
  360.5 10.8 %copy-start.3 = (bf16[3,3,256,256]{3,2,1,0:T(8,128)(2,1)S(1)}, bf16[3,3,256,256]{3,2,1,0:T(8,128)(2,1)}, u32[]{:S(2)}) copy-start(bf16[3,3,256,256]{3,2,1,0:T(8,128)(2,1)} %get-tuple-element.10) | copy-start | bytes 3538948
  362.1 9.9 %collective-permute-start = (bf16[1,256,256]{2,1,0:T(8,128)(2,1)S(1)}, bf16[1,256,256]{2,1,0:T(8,128)(2,1)S(1)}, u32[]{:S(2)}, u32[]{:S(2)}) collective-permute-start(bf16[1,256,256]{2,1,0:T(8,128)(2,1)S(1)} %get-tuple-element.19), channel_id=1, source_target_pairs={{0,1},{1,2},{2,3},{3,4},{4,5},{5,6},{6,7},{7,8},{8,9},{9,10},{10,1... | collective-permute-start | bytes 393224 | tf_op jit(solution)/shard_map/ppermute | solution.py:17
  365.0 9.5 %collective-permute-start.1 = (bf16[1,256,256]{2,1,0:T(8,128)(2,1)S(1)}, bf16[1,256,256]{2,1,0:T(8,128)(2,1)S(1)}, u32[]{:S(2)}, u32[]{:S(2)}) collective-permute-start(bf16[1,256,256]{2,1,0:T(8,128)(2,1)S(1)} %get-tuple-element.20), channel_id=1, source_target_pairs={{1,0},{2,1},{3,2},{4,3},{5,4},{6,5},{7,6},{8,7},{9,8},{10,9},{11,1... | collective-permute-start | bytes 393224 | tf_op jit(solution)/shard_map/ppermute | solution.py:20
  377.7 10.7 %collective-permute-start.2 = (bf16[1,256,256]{2,1,0:T(8,128)(2,1)S(1)}, bf16[1,256,256]{2,1,0:T(8,128)(2,1)S(1)}, u32[]{:S(2)}, u32[]{:S(2)}) collective-permute-start(bf16[1,256,256]{2,1,0:T(8,128)(2,1)S(1)} %get-tuple-element.17), channel_id=1, source_target_pairs={{0,1},{1,2},{2,3},{3,4},{4,5},{5,6},{6,7},{7,8},{8,9},{9,10},{10,1... | collective-permute-start | bytes 393224 | tf_op jit(solution)/shard_map/ppermute | solution.py:17
  379.7 11.0 %collective-permute-start.3 = (bf16[1,256,256]{2,1,0:T(8,128)(2,1)S(1)}, bf16[1,256,256]{2,1,0:T(8,128)(2,1)S(1)}, u32[]{:S(2)}, u32[]{:S(2)}) collective-permute-start(bf16[1,256,256]{2,1,0:T(8,128)(2,1)S(1)} %get-tuple-element.18), channel_id=1, source_target_pairs={{1,0},{2,1},{3,2},{4,3},{5,4},{6,5},{7,6},{8,7},{9,8},{10,9},{11,1... | collective-permute-start | bytes 393224 | tf_op jit(solution)/shard_map/ppermute | solution.py:20
  393.8 10.6 %collective-permute-start.4 = (bf16[1,256,256]{2,1,0:T(8,128)(2,1)S(1)}, bf16[1,256,256]{2,1,0:T(8,128)(2,1)S(1)}, u32[]{:S(2)}, u32[]{:S(2)}) collective-permute-start(bf16[1,256,256]{2,1,0:T(8,128)(2,1)S(1)} %get-tuple-element.15), channel_id=1, source_target_pairs={{0,1},{1,2},{2,3},{3,4},{4,5},{5,6},{6,7},{7,8},{8,9},{9,10},{10,1... | collective-permute-start | bytes 393224 | tf_op jit(solution)/shard_map/ppermute | solution.py:17
  395.7 10.9 %collective-permute-start.5 = (bf16[1,256,256]{2,1,0:T(8,128)(2,1)S(1)}, bf16[1,256,256]{2,1,0:T(8,128)(2,1)S(1)}, u32[]{:S(2)}, u32[]{:S(2)}) collective-permute-start(bf16[1,256,256]{2,1,0:T(8,128)(2,1)S(1)} %get-tuple-element.16), channel_id=1, source_target_pairs={{1,0},{2,1},{3,2},{4,3},{5,4},{6,5},{7,6},{8,7},{9,8},{10,9},{11,1... | collective-permute-start | bytes 393224 | tf_op jit(solution)/shard_map/ppermute | solution.py:20
  408.6 1.6 copy-start.1
Sparse Core Ops, SparseCore 0:
  11.5 74.3 all-gather.1
  99.7 81.8 reduce-scatter.2
  244.7 85.0 reduce-scatter.4
